TPU v7x, 256 devices: a whole 4x4x8 slice. The times are simulated.
256 devices in a mesh: branch: 64 (over z, y, core), col: 4 (over x).
Axes of the slice: x: 4, y: 4, z: 8, core: 2. Of those that a mesh axis runs over, the one named last changes fastest.
Arguments:
- points_x: bfloat16 [524288, 256], P('branch', 'col'), may hold values from -6 to 6
- near_blocks: bfloat16 [2048, 8, 256, 256], P('branch', None, 'col'), may hold values from -0.125 to 0.125
- near_list: int32 [2048, 8], P('branch'), may hold values from 0 to 2047, as said below
- leaf_basis: bfloat16 [2048, 256, 64], P('branch'), may hold values from -0.375 to 0.375
- leaf_transfer: bfloat16 [2048, 64, 64], P('branch'), may hold values from -0.125 to 0.125
- level_transfer: bfloat16 [3, 64, 64, 64], P(None, 'branch'), may hold values from -0.75 to 0.75
- coupling: bfloat16 [64, 8, 64, 64], P('branch'), may hold values from -0.25 to 0.25
- coupling_list: int32 [64, 8], P('branch'), may hold values from 0 to 63, as said below
Outputs:
- near_field: bfloat16 [524288, 256], P('branch', 'col')
- coupled: float32 [64, 64, 256], P('branch', None, 'col')
- upward: float32 [3, 64, 64, 256], P(None, 'branch', None, 'col')
Inputs may be any that keep to these rules, and one draw needn't show every extreme that they name: `near_list`: each entry lies within 2 of its row's leaf index; in every row one entry is the leaf itself and at least two others lie exactly 2 away. `coupling_list`: entry (i, j) is never i, i + 1 or i - 1 modulo 64.
All inputs are finite; a program needn't handle non-finite values.
Results may differ from a plain program's by a relative error of at most 0.0031.
Values may be sent and summed in bfloat16 or wider, within the bound.
No kernel may reach another device: no remote copies, remote signals or barrier semaphores. Data moves between devices by JAX's collectives and lax.ppermute only.
A program may use at most 128 MiB of HBM per device.

v0:
```python
import jax
import jax.numpy as jnp
from jax import lax
from jax.sharding import PartitionSpec as P

HALO_LEAVES = 2


def with_halo(array, sides, width):
    for axis, dim in sides:
        size, length = (lax.axis_size(axis), array.shape[dim])
        up = [(i, (i + 1) % size) for i in range(size - 1)]
        down = [(j, i) for i, j in up]
        last = lax.slice_in_dim(array, length - width, length, axis=dim)
        leading = lax.slice_in_dim(array, 0, width, axis=dim)
        before = lax.ppermute(last, axis, up)
        after = lax.ppermute(leading, axis, down)
        array = jnp.concatenate([before, array, after], axis=dim)
    return array


def from_partner(value, axis, stride):
    mask = 2**stride
    pairs = [(source, source ^ mask) for source in range(lax.axis_size(axis))]
    return lax.ppermute(value, axis, pairs)


def body(
    points_x,
    near_blocks,
    near_list,
    leaf_basis,
    leaf_transfer,
    level_transfer,
    coupling,
    coupling_list,
):
    leaves_here = near_blocks.shape[0]
    leaf = leaf_basis.shape[1]
    width = points_x.shape[1]
    padded = with_halo(points_x, (("branch", 0),), HALO_LEAVES * leaf)
    by_leaf = padded.reshape(-1, leaf, width)
    first_leaf = lax.axis_index("branch") * leaves_here - HALO_LEAVES
    local_ids = near_list - first_leaf
    sources = lax.all_gather(by_leaf, "col", axis=2, tiled=True)[local_ids]
    partial_rows = jnp.einsum(
        "lkrs,lksc->lrc", near_blocks, sources, preferred_element_type=jnp.float32
    ).astype(jnp.bfloat16)
    near_rows = lax.all_to_all(partial_rows, "col", split_axis=2, concat_axis=1, tiled=True)
    near_field = near_rows.reshape(-1, width)
    local_x = points_x.reshape(leaves_here, leaf, width)
    projected = jnp.einsum(
        "lsa,lsc->lac", leaf_basis, local_x, preferred_element_type=jnp.float32
    ).astype(jnp.bfloat16)
    node = jnp.einsum("lab,lac->bc", leaf_transfer, projected, preferred_element_type=jnp.float32)
    terms = jnp.einsum(
        "kab,ac->kbc",
        level_transfer[:, 0].astype(jnp.float32),
        node,
        precision=lax.Precision.HIGHEST,
    )
    levels = terms.shape[0]
    summed = terms
    for bit in range(levels):
        other = from_partner(summed, "branch", bit)
        wanted = (jnp.arange(levels) >= bit)[:, None, None]
        summed = summed + jnp.where(wanted, other, 0.0)
    everyone = lax.all_gather(node[None], "branch", axis=0, tiled=True)
    picked = everyone[coupling_list[0]]
    coupled = jnp.einsum(
        "jab,jbc->ac", coupling[0].astype(jnp.float32), picked, precision=lax.Precision.HIGHEST
    )
    return (near_field, coupled[None], summed[:, None])


def solution(mesh):
    placed = (
        P("branch", "col"),
        P("branch", None, "col", None),
        P("branch", None),
        P("branch", None, None),
        P("branch", None, None),
        P(None, "branch", None, None),
        P("branch", None, None, None),
        P("branch", None),
    )
    return jax.shard_map(
        body,
        mesh=mesh,
        in_specs=placed,
        out_specs=(P("branch", "col"), P("branch", None, "col"), P(None, "branch", None, "col")),
        check_vma=False,
    )
```

profile of v0, /device:TPU:1, one launch (start us, length us, event | category | flops | bytes accessed | tf_op | source)
XLA Modules:
  0.0 181.7 jit_solution(9650892481681377175)
XLA Ops:
  7.2 0.0 copy-start
  7.2 0.0 all-gather.4.cloned.1.call-start
  7.2 1.0 fusion.9
  8.2 5.1 %collective-permute-start.1 = (bf16[512,64]{0,1:T(8,128)(2,1)S(1)}, bf16[512,64]{0,1:T(8,128)(2,1)S(1)}, u32[]{:S(2)}, u32[]{:S(2)}) collective-permute-start(bf16[512,64]{0,1:T(8,128)(2,1)S(1)} %get-tuple-element.13), channel_id=1, source_target_pairs={{4,0},{8,4},{12,8},{16,12},{20,16},{24,20},{28,24},{32,28},{36,32}... | collective-permute-start | bytes 196616 | tf_op jit(solution)/shard_map/ppermute | solution.py:17
  13.3 1.9 %collective-permute-start = (bf16[512,64]{0,1:T(8,128)(2,1)S(1)}, bf16[512,64]{0,1:T(8,128)(2,1)S(1)}, u32[]{:S(2)}, u32[]{:S(2)}) collective-permute-start(bf16[512,64]{0,1:T(8,128)(2,1)S(1)} %get-tuple-element.12), channel_id=1, source_target_pairs={{0,4},{4,8},{8,12},{12,16},{16,20},{20,24},{24,28},{28,32},{32,36}... | collective-permute-start | bytes 196616 | tf_op jit(solution)/shard_map/ppermute | solution.py:16
  15.3 0.0 collective-permute-done.1
  15.3 1.3 collective-permute-done
  16.6 1.3 pad_maximum_fusion
  17.9 0.0 copy-start.2
  17.9 0.0 copy-start.6
  17.9 1.2 copy.44
  19.1 0.0 copy-start.4
  19.1 0.0 copy-start.5
  19.1 0.0 copy-start.7
  19.1 0.0 all-gather.4.cloned.1.call-update
  19.1 0.0 all-gather.6.cloned.1.call-start
  19.2 0.0 copy-done
  19.2 0.2 copy-done.2
  19.5 0.2 copy-done.6
  19.7 0.6 fusion.1
  20.3 0.0 copy-done.4
  20.3 0.2 convolution_bitcast_fusion
  20.5 0.2 collective-permute-start.2
  20.6 0.7 copy.29
  21.3 0.0 all-gather.6.cloned.1.call-update
  21.4 0.0 copy-done.5
  21.4 0.1 copy.23
  21.5 0.1 reshape.57
  21.6 0.0 copy-done.7
  21.6 0.3 collective-permute-done.2
  21.9 2.2 %collective-permute-start.3 = (f32[3,64,64]{1,2,0:T(8,128)S(1)}, f32[3,64,64]{1,2,0:T(8,128)S(1)}, u32[]{:S(2)}, u32[]{:S(2)}) collective-permute-start(f32[3,64,64]{1,2,0:T(8,128)S(1)} %add.29), channel_id=1, source_target_pairs={{0,8},{4,12},{8,0},{12,4},{16,24},{20,28},{24,16},{28,20},{32,40},... | collective-permute-start | bytes 147464 | tf_op jit(solution)/shard_map/ppermute | solution.py:25
  24.1 55.9 %all-gather.4.cloned.1.call-done = bf16[36,256,256]{1,2,0:T(8,128)(2,1)} async-done(((bf16[36,256,64]{1,2,0:T(8,128)(2,1)}), bf16[36,256,256]{1,2,0:T(8,128)(2,1)}) %all-gather.4.cloned.1.call-update) | async-done | bytes 4718608 | tf_op jit(solution)/shard_map/all_gather | solution.py:45
  80.0 6.6 %copy.24 = bf16[36,256,256]{2,1,0:T(8,128)(2,1)} copy(bf16[36,256,256]{1,2,0:T(8,128)(2,1)} %all-gather.4.cloned.1.call-done) | data formatting | bytes 9437184 | tf_op jit(solution)/shard_map/all_gather | solution.py:45
  86.6 16.2 %gather_fusion = bf16[256,256,256]{2,1,0:T(8,128)(2,1)} fusion(bf16[36,256,256]{2,1,0:T(8,128)(2,1)} %copy.24, s32[1024]{0:T(1024)S(1)} %pad_clamp_fusion.1), kind=kCustom, calls=%fused_computation | custom fusion | bytes 67109888 | tf_op jit(solution)/shard_map/gather | solution.py:45
  102.8 16.3 %fusion = bf16[32,64,256]{2,1,0:T(8,128)(2,1)S(1)} fusion(bf16[32,8,64,256]{3,2,1,0:T(8,128)(2,1)} %param.9, bf16[32,8,256,256]{3,2,1,0:T(8,128)(2,1)} %bitcast.54), kind=kOutput, calls=%fused_computation.3 | convolution fusion | flops 2148007936 | bytes 42991616 | tf_op jit(solution)/shard_map/lkrs,lksc->lrc/dot_general | solution.py:46
  119.1 3.1 %copy.25 = bf16[32,64,256]{1,0,2:T(8,128)(2,1)S(1)} copy(bf16[32,64,256]{2,1,0:T(8,128)(2,1)S(1)} %fusion) | data formatting | bytes 2097152 | tf_op jit(solution)/shard_map/convert_element_type | solution.py:48
  122.2 2.7 %reshape.78 = bf16[4,2,65536]{2,1,0:T(2,128)(2,1)} reshape(bf16[256,32,64]{2,1,0:T(8,128)(2,1)S(1)} %bitcast.55) | data formatting | bytes 2097152
  124.8 0.0 copy-start.3
  124.8 3.6 %all-to-all-start = ((bf16[4,2,65536]{2,1,0:T(2,128)(2,1)}), bf16[4,2,65536]{2,1,0:T(2,128)(2,1)S(1)}, u32[]{:S(2)}, u32[]{:S(2)}) async-start(bf16[4,2,65536]{2,1,0:T(2,128)(2,1)} %reshape.78), calls=%async_computation | async-start | bytes 2097152 | tf_op jit(solution)/shard_map/all_to_all | solution.py:49
  128.5 0.0 collective-permute-done.3
  128.5 0.1 select_add_fusion
  128.6 3.0 %collective-permute-start.4 = (f32[3,64,64]{1,2,0:T(8,128)S(1)}, f32[3,64,64]{1,2,0:T(8,128)S(1)}, u32[]{:S(2)}, u32[]{:S(2)}) collective-permute-start(f32[3,64,64]{1,2,0:T(8,128)S(1)} %select_add_fusion), channel_id=1, source_target_pairs={{0,16},{4,20},{8,24},{12,28},{16,0},{20,4},{24,8},{28,12},{32,48},... | collective-permute-start | bytes 147464 | tf_op jit(solution)/shard_map/ppermute | solution.py:25
  131.6 2.9 %collective-permute-done.4 = f32[3,64,64]{1,2,0:T(8,128)S(1)} collective-permute-done((f32[3,64,64]{1,2,0:T(8,128)S(1)}, f32[3,64,64]{1,2,0:T(8,128)S(1)}, u32[]{:S(2)}, u32[]{:S(2)}) %collective-permute-start.4) | collective-permute-done | bytes 49184 | tf_op jit(solution)/shard_map/ppermute | solution.py:25
  134.5 0.1 add_bitcast_fusion
  134.6 0.7 copy.32
  135.3 26.2 %all-gather.6.cloned.1.call-done = f32[4096,64]{1,0:T(8,128)} async-done(((f32[64,64]{1,0:T(8,128)}), f32[4096,64]{1,0:T(8,128)}) %all-gather.6.cloned.1.call-update) | async-done | bytes 1048592 | tf_op jit(solution)/shard_map/all_gather | solution.py:68
  161.6 2.2 %gather_fusion.1 = f32[8,64,64]{2,1,0:T(8,128)S(1)} fusion(f32[64,64,64]{2,1,0:T(8,128)} %bitcast.61, s32[1024]{0:T(1024)S(1)} %pad_clamp_fusion), kind=kCustom, calls=%fused_computation.1 | custom fusion | bytes 262176 | tf_op jit(solution)/shard_map/gather | solution.py:69
  163.7 0.0 copy-done.3
  163.7 0.4 convolution_bitcast_fusion.1
  164.1 0.7 copy.31
  164.8 0.0 all-to-all-done
  164.8 1.4 reshape.79
  166.2 0.0 copy-start.1
  166.3 4.0 %copy.26 = bf16[32,4,64,64]{2,1,0,3:T(4,128)(2,1)} copy(bf16[32,4,64,64]{2,0,3,1:T(8,128)(2,1)S(1)} %bitcast.56) | data formatting | bytes 2097152 | tf_op jit(solution)/shard_map/all_to_all | solution.py:49
  170.3 4.6 %reshape.53 = bf16[8192,64]{0,1:T(8,128)(2,1)} reshape(bf16[32,4,64,64]{2,1,0,3:T(4,128)(2,1)} %copy.26) | data formatting | bytes 2097152 | tf_op jit(solution)/shard_map/reshape | solution.py:50
  174.9 0.0 copy-done.1
  (7 shorter events, 0.1 us)
Async XLA Ops:
  7.2 12.0 %copy-start = (bf16[32,256,64]{1,2,0:T(8,128)(2,1)S(1)}, bf16[32,256,64]{1,2,0:T(8,128)(2,1)}, u32[]{:S(2)}) copy-start(bf16[32,256,64]{1,2,0:T(8,128)(2,1)} %param.11) | copy-start | bytes 3145732
  7.2 72.8 %all-gather.4.cloned.1.call-start = ((), (), s32[]{:S(2)}) async-start(), calls=%async_computation.1 | async-start | bytes 5898240 | tf_op jit(solution)/shard_map/all_gather | solution.py:45
  8.2 7.1 %collective-permute-start.1 = (bf16[512,64]{0,1:T(8,128)(2,1)S(1)}, bf16[512,64]{0,1:T(8,128)(2,1)S(1)}, u32[]{:S(2)}, u32[]{:S(2)}) collective-permute-start(bf16[512,64]{0,1:T(8,128)(2,1)S(1)} %get-tuple-element.13), channel_id=1, source_target_pairs={{4,0},{8,4},{12,8},{16,12},{20,16},{24,20},{28,24},{32,28},{36,32}... | collective-permute-start | bytes 196616 | tf_op jit(solution)/shard_map/ppermute | solution.py:17
  13.3 3.2 %collective-permute-start = (bf16[512,64]{0,1:T(8,128)(2,1)S(1)}, bf16[512,64]{0,1:T(8,128)(2,1)S(1)}, u32[]{:S(2)}, u32[]{:S(2)}) collective-permute-start(bf16[512,64]{0,1:T(8,128)(2,1)S(1)} %get-tuple-element.12), channel_id=1, source_target_pairs={{0,4},{4,8},{8,12},{12,16},{16,20},{20,24},{24,28},{28,32},{32,36}... | collective-permute-start | bytes 196616 | tf_op jit(solution)/shard_map/ppermute | solution.py:16
  17.9 1.6 copy-start.2
  17.9 1.8 copy-start.6
  19.1 1.2 copy-start.4
  19.1 2.2 %copy-start.5 = (s32[32,8]{0,1:T(8,128)S(1)}, s32[32,8]{0,1:T(8,128)}, u32[]{:S(2)}) copy-start(s32[32,8]{0,1:T(8,128)} %param.10) | copy-start | bytes 3076
  19.1 2.4 %copy-start.7 = (s32[1,8]{1,0:T(1,128)S(1)}, s32[1,8]{1,0:T(1,128)}, u32[]{:S(2)}) copy-start(s32[1,8]{1,0:T(1,128)} %param.15) | copy-start | bytes 100
  19.1 142.4 %all-gather.6.cloned.1.call-start = ((), (), s32[]{:S(2)}) async-start(), calls=%async_computation.2 | async-start | bytes 2129920 | tf_op jit(solution)/shard_map/all_gather | solution.py:68
  20.5 1.4 collective-permute-start.2
  21.9 106.6 %collective-permute-start.3 = (f32[3,64,64]{1,2,0:T(8,128)S(1)}, f32[3,64,64]{1,2,0:T(8,128)S(1)}, u32[]{:S(2)}, u32[]{:S(2)}) collective-permute-start(f32[3,64,64]{1,2,0:T(8,128)S(1)} %add.29), channel_id=1, source_target_pairs={{0,8},{4,12},{8,0},{12,4},{16,24},{20,28},{24,16},{28,20},{32,40},... | collective-permute-start | bytes 147464 | tf_op jit(solution)/shard_map/ppermute | solution.py:25
  124.8 38.9 %copy-start.3 = (bf16[1,8,64,64]{3,2,1,0:T(8,128)(2,1)S(1)}, bf16[1,8,64,64]{3,2,1,0:T(8,128)(2,1)}, u32[]{:S(2)}) copy-start(bf16[1,8,64,64]{3,2,1,0:T(8,128)(2,1)} %param.14) | copy-start | bytes 196612
  124.8 40.0 %all-to-all-start = ((bf16[4,2,65536]{2,1,0:T(2,128)(2,1)}), bf16[4,2,65536]{2,1,0:T(2,128)(2,1)S(1)}, u32[]{:S(2)}, u32[]{:S(2)}) async-start(bf16[4,2,65536]{2,1,0:T(2,128)(2,1)} %reshape.78), calls=%async_computation | async-start | bytes 2097152 | tf_op jit(solution)/shard_map/all_to_all | solution.py:49
  128.6 5.9 %collective-permute-start.4 = (f32[3,64,64]{1,2,0:T(8,128)S(1)}, f32[3,64,64]{1,2,0:T(8,128)S(1)}, u32[]{:S(2)}, u32[]{:S(2)}) collective-permute-start(f32[3,64,64]{1,2,0:T(8,128)S(1)} %select_add_fusion), channel_id=1, source_target_pairs={{0,16},{4,20},{8,24},{12,28},{16,0},{20,4},{24,8},{28,12},{32,48},... | collective-permute-start | bytes 147464 | tf_op jit(solution)/shard_map/ppermute | solution.py:25
  166.2 8.6 %copy-start.1 = (bf16[32,256,64]{1,2,0:T(8,128)(2,1)S(1)}, bf16[32,256,64]{1,2,0:T(8,128)(2,1)}, u32[]{:S(2)}) copy-start(bf16[32,256,64]{1,2,0:T(8,128)(2,1)} %param.11) | copy-start | bytes 3145732
Sparse Core Ops, SparseCore 0:
  19.3 60.6 all-gather.3
  83.3 78.1 all-gather.5
where the time goes:
time: 182 us
  waiting for transfers between devices  86.6 us (48%)
  local copies, waits for them, and re-layouts  45.7 us (25%)
  matrix products  17.4 us (10%)
  starting transfers between devices  16.2 us (9%)
  between operations  14.3 us (8%)
    all_gather x1, waiting for transfers between devices, body(): sources = lax.all_gather(by_leaf, 'col', axis=2, tiled=True)[local_ids]  55.9 us
    all_gather x1, waiting for transfers between devices, body(): everyone = lax.all_gather(node[None], 'branch', axis=0, tiled=True)  26.2 us
    dot_general x1, matrix products, body(): jnp.einsum('lkrs,lksc->lrc', near_blocks, sources, preferred_element_type...  16.3 us
    gather x1, local copies, waits for them, and re-layouts, body(): sources = lax.all_gather(by_leaf, 'col', axis=2, tiled=True)[local_ids]  16.2 us
    all_gather x1, local copies, waits for them, and re-layouts, body(): sources = lax.all_gather(by_leaf, 'col', axis=2, tiled=True)[local_ids]  6.61 us
    unnamed x20, local copies, waits for them, and re-layouts  6.04 us
    ppermute x3, starting transfers between devices, from_partner(): return lax.ppermute(value, axis, pairs)  5.41 us
    ppermute x1, starting transfers between devices, with_halo(): after = lax.ppermute(leading, axis, down)  5.15 us
  transfers between devices with their start and end apart: 8, of which 5 were waited for; matrix products, arithmetic and copies ran while one was open for 28% of the time, Pallas kernels for 0%

commit v1 on v0

v1 whole, which is shorter than its diff:
```python
import functools

import jax
import jax.numpy as jnp
from jax import lax
from jax.experimental import pallas as pl
from jax.experimental.pallas import tpu as pltpu
from jax.sharding import PartitionSpec as P

HALO_LEAVES = 2
PARTS = 4
VMEM_LIMIT = 16 << 20
NT = (((1,), (1,)), ((), ()))
F32 = jnp.float32
BF16 = jnp.bfloat16


def shifted(value, axis, step):
    size = lax.axis_size(axis)
    return lax.ppermute(value, axis, [(i, (i + step) % size) for i in range(size)])


def along_branch(value, step):
    size = lax.axis_size("branch")
    pairs = [(i, i + step) for i in range(size) if 0 <= i + step < size]
    return lax.ppermute(value, "branch", pairs)


def near_kernel(pieces, count, out_rows, steps, ids_ref, blocks_ref, *refs):
    ins, outs = refs[:count], refs[count : count + len(out_rows)]
    held, sems = refs[count + len(out_rows) :]
    step = pl.program_id(0)
    leaves, blocks, rows, leaf = blocks_ref.shape

    @pl.when(step == 0)
    def load():
        copies = []
        for n, (source, row, rows_of, at, lane, wide) in enumerate(pieces):
            taken = ins[source].at[row : row + rows_of, lane : lane + wide]
            place = held.at[at[0] : at[0] + rows_of, at[1] : at[1] + wide]
            copies.append(pltpu.make_async_copy(taken, place, sems.at[n]))
        for copy in copies:
            copy.start()
        for copy in copies:
            copy.wait()

    first = lax.axis_index("branch") * (leaves * steps) - HALO_LEAVES
    for pair in range(0, leaves, 2):
        sums = []
        for l in (pair, pair + 1):
            total = None
            for k in range(blocks):
                source = ids_ref[k, step * leaves + l] - first
                lanes = pl.ds(pl.multiple_of(source * leaf, leaf), leaf)
                part = lax.dot_general(
                    held[:, lanes], blocks_ref[l, k], NT, preferred_element_type=F32
                )
                total = part if total is None else total + part
            sums.append(total)
        both = jnp.concatenate(sums, axis=1).astype(BF16)
        row = 0
        for high, out in zip(out_rows, outs):
            out[:, pair * rows : (pair + 2) * rows] = both[row : row + high]
            row += high


def near_rows(ids, near_blocks, pieces, arrays, out_rows, name):
    all_leaves, blocks, rows, leaf = near_blocks.shape
    leaves = 8
    steps = all_leaves // leaves
    columns = sum(out_rows)
    return pl.pallas_call(
        functools.partial(near_kernel, pieces, len(arrays), out_rows, steps),
        grid_spec=pltpu.PrefetchScalarGridSpec(
            num_scalar_prefetch=1,
            grid=(steps,),
            in_specs=[pl.BlockSpec((leaves, blocks, rows, leaf), lambda i, _: (i, 0, 0, 0))]
            + [pl.BlockSpec(memory_space=pl.ANY)] * len(arrays),
            out_specs=[pl.BlockSpec((high, leaves * rows), lambda i, _: (0, i)) for high in out_rows],
            scratch_shapes=[
                pltpu.VMEM((columns, (all_leaves + 2 * HALO_LEAVES) * leaf), BF16),
                pltpu.SemaphoreType.DMA((len(pieces),)),
            ],
        ),
        out_shape=[jax.ShapeDtypeStruct((high, all_leaves * rows), BF16) for high in out_rows],
        compiler_params=pltpu.CompilerParams(vmem_limit_bytes=VMEM_LIMIT),
        cost_estimate=pl.CostEstimate(
            flops=2 * columns * all_leaves * blocks * rows * leaf,
            bytes_accessed=near_blocks.size * 2,
            transcendentals=0,
        ),
        name=name,
    )(ids, near_blocks, *arrays)


def assemble_kernel(places, *refs):
    ins, out = refs[:-3], refs[-3]
    held, sems = refs[-2:]
    step = pl.program_id(0)
    me = lax.axis_index("col")
    rows = 64
    wide = out.shape[1] // PARTS

    @pl.when(step == 0)
    def load():
        copies = []
        for n, (ahead, row) in enumerate(places):
            part = lax.rem(me + ahead, PARTS)
            place = held.at[part, row : row + ins[n].shape[0], :]
            copies.append(pltpu.make_async_copy(ins[n], place, sems.at[n]))
        for copy in copies:
            copy.start()
        for copy in copies:
            copy.wait()

    for pair in range(wide // (2 * rows)):
        lanes = pl.ds(pl.multiple_of(step * wide + pair * 2 * rows, 2 * rows), 2 * rows)
        parts = [held[p, :, lanes] for p in range(PARTS)]
        for l in range(2):
            at = (2 * pair + l) * PARTS * rows
            halves = [part[:, l * rows : (l + 1) * rows] for part in parts]
            out[:, at : at + 2 * rows] = jnp.concatenate(halves[:2], axis=1)
            out[:, at + 2 * rows : at + 4 * rows] = jnp.concatenate(halves[2:], axis=1)


def assemble(places, arrays, columns, points):
    steps = 4
    return pl.pallas_call(
        functools.partial(assemble_kernel, places),
        grid=(steps,),
        in_specs=[pl.BlockSpec(memory_space=pl.ANY)] * len(arrays),
        out_specs=pl.BlockSpec((columns, points // steps), lambda i: (0, i)),
        scratch_shapes=[
            pltpu.VMEM((PARTS, columns, points // PARTS), BF16),
            pltpu.SemaphoreType.DMA((len(places),)),
        ],
        out_shape=jax.ShapeDtypeStruct((columns, points), BF16),
        compiler_params=pltpu.CompilerParams(vmem_limit_bytes=VMEM_LIMIT),
        name="assemble",
    )(*arrays)


def coupled_kernel(list_ref, coupling_ref, everyone, out, held, sems):
    count, rank = coupling_ref.shape[:2]
    copies = [
        pltpu.make_async_copy(everyone.at[list_ref[0, j]], held.at[j], sems.at[j]) for j in range(count)
    ]
    for copy in copies:
        copy.start()
    for copy in copies:
        copy.wait()
    total = jnp.zeros(out.shape, F32)
    for j in range(count):
        packed = held[j]
        node = jnp.concatenate([packed[:, :rank], packed[:, rank:]], axis=0)
        total += jnp.dot(
            coupling_ref[j].astype(F32), node, precision=lax.Precision.HIGHEST, preferred_element_type=F32
        )
    out[...] = total


def coupled_rows(coupling_list, coupling, everyone):
    count, rank = coupling.shape[:2]
    return pl.pallas_call(
        coupled_kernel,
        in_specs=[
            pl.BlockSpec(memory_space=pltpu.SMEM),
            pl.BlockSpec(memory_space=pltpu.VMEM),
            pl.BlockSpec(memory_space=pl.ANY),
        ],
        out_specs=pl.BlockSpec(memory_space=pltpu.VMEM),
        scratch_shapes=[
            pltpu.VMEM((count,) + everyone.shape[1:], F32),
            pltpu.SemaphoreType.DMA((count,)),
        ],
        out_shape=jax.ShapeDtypeStruct((rank, rank), F32),
        name="coupled",
    )(coupling_list, coupling, everyone)


def body(
    points_x,
    near_blocks,
    near_list,
    leaf_basis,
    leaf_transfer,
    level_transfer,
    coupling,
    coupling_list,
):
    leaves_here = near_blocks.shape[0]
    leaf = leaf_basis.shape[1]
    points, width = points_x.shape
    edge = HALO_LEAVES * leaf
    half = width // 2
    columns = points_x.T
    ids = near_list.T
    low, high = columns[:half], columns[half:]

    left_low = shifted(low, "col", 1)
    right_high = shifted(high, "col", -1)
    before = along_branch(columns[:, points - edge :], 1)
    after = along_branch(columns[:, :edge], -1)
    edges = jnp.concatenate([before, after], axis=1)
    left_rest = shifted(jnp.concatenate([high, edges[half:], edges[:half]], axis=1), "col", 1)
    right_rest = shifted(jnp.concatenate([low, edges[:half], edges[half:]], axis=1), "col", -1)
    far_edges = shifted(edges, "col", 2)
    far_low = shifted(left_low, "col", 1)
    far_high = shifted(right_high, "col", -1)

    local_x = points_x.reshape(leaves_here, leaf, width)
    projected = jnp.einsum("lsa,lsc->lac", leaf_basis, local_x, preferred_element_type=F32).astype(BF16)
    node = jnp.einsum("lab,lac->bc", leaf_transfer, projected, preferred_element_type=F32)
    rank = node.shape[0]
    packed = jnp.concatenate([node[: rank // 2], node[rank // 2 :]], axis=1)
    copies = jnp.broadcast_to(packed[None], (lax.axis_size("branch"),) + packed.shape)
    everyone = lax.all_to_all(copies, "branch", split_axis=0, concat_axis=0, tiled=True)
    terms = jnp.einsum(
        "kab,ac->kbc",
        level_transfer[:, 0].astype(F32),
        node,
        precision=lax.Precision.HIGHEST,
    )
    levels = []
    summed = terms
    for bit in range(terms.shape[0]):
        pairs = [(i, i ^ 2**bit) for i in range(lax.axis_size("branch"))]
        summed = summed + lax.ppermute(summed, "branch", pairs)
        levels.append(summed[0])
        summed = summed[1:]
    upward = jnp.stack(levels)[:, None]

    end = edge + points
    (own,) = near_rows(
        ids,
        near_blocks,
        [(0, 0, width, (0, 0), 0, edge), (0, 0, width, (0, end), edge, edge), (1, 0, width, (0, edge), 0, points)],
        [edges, columns, left_low, right_high],
        [width],
        "near_own",
    )
    pieces = []
    for n, top in ((0, 0), (2, width)):
        swap = half if n else 0
        main, other = top + swap, top + half - swap
        pieces += [
            (n, 0, half, (main, edge), 0, points),
            (n + 1, 0, half, (main, 0), points + 2 * edge, edge),
            (n + 1, 0, half, (main, end), points + 3 * edge, edge),
            (n + 1, 0, half, (other, edge), 0, points),
            (n + 1, 0, half, (other, 0), points, edge),
            (n + 1, 0, half, (other, end), points + edge, edge),
        ]
    to_left, to_right = near_rows(
        ids, near_blocks, pieces, [left_low, left_rest, right_high, right_rest], [width] * 2, "near_sides"
    )
    (to_far,) = near_rows(
        ids,
        near_blocks,
        [
            (0, 0, width, (0, 0), 0, edge),
            (0, 0, width, (0, end), edge, edge),
            (1, 0, half, (0, edge), 0, points),
            (2, 0, half, (half, edge), 0, points),
        ],
        [far_edges, far_low, far_high],
        [width],
        "near_far",
    )
    from_right = shifted(to_left, "col", -1)
    from_left = shifted(to_right, "col", 1)
    from_far = shifted(to_far, "col", 2)
    coupled = coupled_rows(coupling_list, coupling[0], everyone)
    near_field = assemble(
        [(0, 0), (1, 0), (3, 0), (2, 0)], [own, from_right, from_left, from_far, coupled, upward], width, points
    )
    return (near_field.T, coupled[None], upward)


def solution(mesh):
    placed = (
        P("branch", "col"),
        P("branch", None, "col", None),
        P("branch", None),
        P("branch", None, None),
        P("branch", None, None),
        P(None, "branch", None, None),
        P("branch", None, None, None),
        P("branch", None),
    )
    return jax.shard_map(
        body,
        mesh=mesh,
        in_specs=placed,
        out_specs=(P("branch", "col"), P("branch", None, "col"), P(None, "branch", None, "col")),
        check_vma=False,
    )
```

time: 182 us -> 81.5 us (0.45)
  waiting for transfers between devices: 86.6 us -> 8.83 us
  local copies, waits for them, and re-layouts: 45.7 us -> 8.59 us
  Pallas kernels: 0 us -> 21.5 us
  starting transfers between devices: 16.2 us -> 36.7 us
  matrix products: 17.4 us -> 1.84 us
  between operations: 14.3 us -> 1.08 us
    all_gather x2 -> x0, waiting for transfers between devices: 82.1 us -> none  [the longest x1 55.9 us: body(): sources = lax.all_gather(by_leaf, 'col', axis=2, tiled=True)[local_ids]]
    pallas_call x0 -> x5, Pallas kernels: none -> 21.5 us  [the longest x3 15.6 us: near_rows(): pl.pallas_call(functools.partial(near_kernel, pieces, len(arrays), out_ro...]
    gather x2 -> x0, local copies, waits for them, and re-layouts: 18.3 us -> none  [the longest x1 16.2 us: body(): sources = lax.all_gather(by_leaf, 'col', axis=2, tiled=True)[local_ids]]
    dot_general x3 -> x1, matrix products: 16.8 us -> 0.25 us  [body(): jnp.einsum('kab,ac->kbc', level_transfer[:, 0].astype(F32), node, precisi...]
    ppermute x5 -> x15, starting transfers between devices: 12.5 us -> 23 us  [the longest x10 10.4 us: shifted(): lax.ppermute(value, axis, [(i, (i + step) % size) for i in range(size)])]
    all_to_all x1, starting transfers between devices: 3.65 us -> 13.6 us  [body(): lax.all_to_all(copies, 'branch', split_axis=0, concat_axis=0, tiled=True)]
    all_gather x1 -> x0, local copies, waits for them, and re-layouts: 6.61 us -> none  [body(): sources = lax.all_gather(by_leaf, 'col', axis=2, tiled=True)[local_ids]]
    reshape x2 -> x0, local copies, waits for them, and re-layouts: 5.79 us -> none  [the longest x1 4.59 us: body(): near_field = near_rows.reshape(-1, width)]
  transfers between devices with their start and end apart: 8 -> 16, of which waited for: 5 -> 4; matrix products, arithmetic and copies ran while one was open for 28% -> 8% of each run, Pallas kernels for 0% -> 23%
where the time goes in v1:
time: 81.5 us; the launch traced here: 79.9 us
  starting transfers between devices  36.7 us (45%)
  Pallas kernels  21.5 us (26%)
  waiting for transfers between devices  8.83 us (11%)
  local copies, waits for them, and re-layouts  8.59 us (11%)
  matrix products  1.84 us (2%)
  other arithmetic  1.42 us (2%)
  between operations  1.08 us (1%)
    pallas_call x3, Pallas kernels, near_rows(): pl.pallas_call(functools.partial(near_kernel, pieces, len(arrays), out_ro...  15.6 us
    all_to_all x1, starting transfers between devices, body(): lax.all_to_all(copies, 'branch', split_axis=0, concat_axis=0, tiled=True)  13.6 us
    ppermute x10, starting transfers between devices, shifted(): lax.ppermute(value, axis, [(i, (i + step) % size) for i in range(size)])  10.4 us
    ppermute x2, starting transfers between devices, along_branch(): return lax.ppermute(value, 'branch', pairs)  6.52 us
    ppermute x3, starting transfers between devices, body(): summed = summed + lax.ppermute(summed, 'branch', pairs)  6.12 us
    ppermute x10, waiting for transfers between devices, shifted(): lax.ppermute(value, axis, [(i, (i + step) % size) for i in range(size)])  4.63 us
    ppermute x3, waiting for transfers between devices, body(): summed = summed + lax.ppermute(summed, 'branch', pairs)  4.19 us
    unnamed x17, local copies, waits for them, and re-layouts  4.18 us
  transfers between devices with their start and end apart: 16, of which 4 were waited for; matrix products, arithmetic and copies ran while one was open for 8% of the time, Pallas kernels for 23%

profile of v1, /device:TPU:1, one launch (start us, length us, event | category | flops | bytes accessed | tf_op | source)
XLA Modules:
  0.0 79.9 jit_solution(17967956131729103914)
XLA Ops:
  0.6 0.0 copy-start
  0.6 0.0 copy-start.2
  0.7 1.0 %fusion.7 = (bf16[64,512]{1,0:T(8,128)(2,1)S(1)}, bf16[64,512]{1,0:T(8,128)(2,1)S(1)}) fusion(bf16[64,8192]{1,0:T(8,128)(2,1)} %bitcast.25), kind=kLoop, calls=%fused_computation.15 | loop fusion | bytes 262144 | tf_op jit(solution)/shard_map/slice | solution.py:203
  1.7 4.6 %collective-permute-start = (bf16[64,512]{1,0:T(8,128)(2,1)S(1)}, bf16[64,512]{1,0:T(8,128)(2,1)S(1)}, u32[]{:S(2)}, u32[]{:S(2)}) collective-permute-start(bf16[64,512]{1,0:T(8,128)(2,1)S(1)} %get-tuple-element.10), channel_id=1, source_target_pairs={{0,4},{4,8},{8,12},{12,16},{16,20},{20,24},{24,28},{28,32},{32,36}... | collective-permute-start | bytes 196616 | tf_op jit(solution)/shard_map/ppermute | solution.py:26
  6.3 1.9 %collective-permute-start.1 = (bf16[64,512]{1,0:T(8,128)(2,1)S(1)}, bf16[64,512]{1,0:T(8,128)(2,1)S(1)}, u32[]{:S(2)}, u32[]{:S(2)}) collective-permute-start(bf16[64,512]{1,0:T(8,128)(2,1)S(1)} %get-tuple-element.9), channel_id=1, source_target_pairs={{4,0},{8,4},{12,8},{16,12},{20,16},{24,20},{28,24},{32,28},{36,32}... | collective-permute-start | bytes 196616 | tf_op jit(solution)/shard_map/ppermute | solution.py:26
  8.2 2.2 %fusion.6 = (bf16[32,8192]{1,0:T(8,128)(2,1)}, bf16[32,8192]{1,0:T(8,128)(2,1)}) fusion(bf16[64,8192]{1,0:T(8,128)(2,1)} %bitcast.26), kind=kLoop, calls=%fused_computation.14 | loop fusion | bytes 2097152 | tf_op jit(solution)/shard_map/slice | solution.py:198
  10.5 1.2 %collective-permute-start.2 = (bf16[32,8192]{1,0:T(8,128)(2,1)}, bf16[32,8192]{1,0:T(8,128)(2,1)S(1)}, u32[]{:S(2)}, u32[]{:S(2)}) collective-permute-start(bf16[32,8192]{1,0:T(8,128)(2,1)} %get-tuple-element.8), channel_id=1, source_target_pairs={{0,1},{1,2},{2,3},{3,0},{4,5},{5,6},{6,7},{7,4},{8,9},{9,10},{10,1... | collective-permute-start | bytes 1572872 | tf_op jit(solution)/shard_map/ppermute | solution.py:20
  11.7 1.5 %collective-permute-start.3 = (bf16[32,8192]{1,0:T(8,128)(2,1)}, bf16[32,8192]{1,0:T(8,128)(2,1)S(1)}, u32[]{:S(2)}, u32[]{:S(2)}) collective-permute-start(bf16[32,8192]{1,0:T(8,128)(2,1)} %get-tuple-element.7), channel_id=1, source_target_pairs={{0,3},{1,0},{2,1},{3,2},{4,7},{5,4},{6,5},{7,6},{8,11},{9,8},{10,9... | collective-permute-start | bytes 1572872 | tf_op jit(solution)/shard_map/ppermute | solution.py:20
  13.1 0.0 copy-done
  13.1 0.0 copy-done.2
  13.1 1.6 %fusion = f32[64,64,1]{0,1,2:T(8,128)S(1)} fusion(bf16[32,64,64]{2,1,0:T(8,128)(2,1)} %param.12, bf16[32,256,64]{1,2,0:T(8,128)(2,1)S(1)} %copy-done, bf16[8,32,8,256]{3,2,1,0:T(8,128)(2,1)S(1)} %bitcast.27), kind=kOutput, calls=%fused_computation.1 | convolution fusion | flops 84017152 | bytes 2375680 | tf_op jit(solution)/shard_map/lab,lac->bc/dot_general | solution.py:213
  14.8 0.1 pad_maximum_fusion.2
  14.8 1.1 %broadcast_in_dim.12 = f32[64,32,128]{2,1,0:T(8,128)} broadcast(f32[32,128]{1,0:T(8,128)S(1)} %pad_maximum_fusion.2), dimensions={1,2} | broadcast | bytes 1064960 | tf_op jit(solution)/shard_map/broadcast_in_dim | solution.py:216
  15.9 13.6 %all-to-all-start = ((f32[64,32,128]{2,1,0:T(8,128)}), f32[64,32,128]{2,1,0:T(8,128)}, u32[]{:S(2)}, u32[]{:S(2)}) async-start(f32[64,32,128]{2,1,0:T(8,128)} %broadcast_in_dim.12), calls=%async_computation | async-start | bytes 2097152 | tf_op jit(solution)/shard_map/all_to_all | solution.py:217
  29.6 0.0 collective-permute-done
  29.6 0.0 collective-permute-done.1
  29.7 0.0 copy-start.7
  29.7 0.0 copy-start.5
  29.7 1.3 %pad_maximum_fusion.1 = (bf16[32,10240]{1,0:T(8,128)(2,1)S(1)}, bf16[32,10240]{1,0:T(8,128)(2,1)S(1)}) fusion(bf16[32,1024]{1,0:T(8,128)(2,1)S(1)} %get-tuple-element.13, bf16[32,1024]{1,0:T(8,128)(2,1)S(1)} %get-tuple-element.14, bf16[32,8192]{1,0:T(8,128)(2,1)} %get-tuple-element.8, bf16[32,8192]{1,0:T(8,128)(2,1)} %get-tuple-element.7), kind=kLoop, calls=%fused_computation.6 | loop fusion | flops 3932160 | bytes 2490368 | tf_op jit(solution)/shard_map/concatenate | solution.py:206
  31.0 0.1 collective-permute-start.4
  31.1 2.7 %collective-permute-start.5 = (bf16[32,10240]{1,0:T(8,128)(2,1)S(1)}, bf16[32,10240]{1,0:T(8,128)(2,1)S(1)}, u32[]{:S(2)}, u32[]{:S(2)}) collective-permute-start(bf16[32,10240]{1,0:T(8,128)(2,1)S(1)} %get-tuple-element.11), channel_id=1, source_target_pairs={{0,3},{1,0},{2,1},{3,2},{4,7},{5,4},{6,5},{7,6},{8,11},{9,8},{10,9... | collective-permute-start | bytes 1966088 | tf_op jit(solution)/shard_map/ppermute | solution.py:20
  33.8 0.0 collective-permute-done.3.refs_3_.refs_2_
  33.8 0.1 collective-permute-start.10
  33.8 0.0 collective-permute-done.2.refs_2_.refs_0_
  33.8 1.4 %collective-permute-start.9 = (bf16[32,8192]{1,0:T(8,128)(2,1)S(1)}, bf16[32,8192]{1,0:T(8,128)(2,1)S(1)}, u32[]{:S(2)}, u32[]{:S(2)}) collective-permute-start(bf16[32,8192]{1,0:T(8,128)(2,1)S(1)} %collective-permute-done.2.refs_2_.refs_0_), channel_id=1, source_target_pairs={{0,1},{1,2},{2,3},{3,0},{4,5},{5,6},{6,7},{7,4},{8,9},{9,10},{10,1... | collective-permute-start | bytes 1572872 | tf_op jit(solution)/shard_map/ppermute | solution.py:20
  35.2 0.0 copy-done.7
  35.2 0.2 convolution_bitcast_fusion
  35.5 1.7 %collective-permute-start.12 = (f32[3,64,64]{2,1,0:T(8,128)S(1)}, f32[3,64,64]{2,1,0:T(8,128)S(1)}, u32[]{:S(2)}, u32[]{:S(2)}) collective-permute-start(f32[3,64,64]{2,1,0:T(8,128)S(1)} %convolution_bitcast_fusion), channel_id=1, source_target_pairs={{0,4},{4,0},{8,12},{12,8},{16,20},{20,16},{24,28},{28,24},{32,36},... | collective-permute-start | bytes 147464 | tf_op jit(solution)/shard_map/ppermute | solution.py:228
  37.2 0.9 %collective-permute-done.12 = f32[3,64,64]{2,1,0:T(8,128)S(1)} collective-permute-done((f32[3,64,64]{2,1,0:T(8,128)S(1)}, f32[3,64,64]{2,1,0:T(8,128)S(1)}, u32[]{:S(2)}, u32[]{:S(2)}) %collective-permute-start.12) | collective-permute-done | bytes 49184 | tf_op jit(solution)/shard_map/ppermute | solution.py:228
  38.2 0.0 copy-start.6
  38.2 1.3 %collective-permute-start.13 = (f32[2,64,64]{2,1,0:T(8,128)S(1)}, f32[2,64,64]{2,1,0:T(8,128)S(1)}, u32[]{:S(2)}, u32[]{:S(2)}) collective-permute-start(f32[2,64,64]{2,1,0:T(8,128)S(1)} %slice.59), channel_id=1, source_target_pairs={{0,8},{4,12},{8,0},{12,4},{16,24},{20,28},{24,16},{28,20},{32,40},... | collective-permute-start | bytes 98312 | tf_op jit(solution)/shard_map/ppermute | solution.py:228
  39.5 3.2 %collective-permute-done.13 = f32[2,64,64]{2,1,0:T(8,128)S(1)} collective-permute-done((f32[2,64,64]{2,1,0:T(8,128)S(1)}, f32[2,64,64]{2,1,0:T(8,128)S(1)}, u32[]{:S(2)}, u32[]{:S(2)}) %collective-permute-start.13) | collective-permute-done | bytes 32800 | tf_op jit(solution)/shard_map/ppermute | solution.py:228
  42.8 0.8 %collective-permute-start.8 = (bf16[64,1024]{1,0:T(8,128)(2,1)S(1)}, bf16[64,1024]{1,0:T(8,128)(2,1)S(1)}, u32[]{:S(2)}, u32[]{:S(2)}) collective-permute-start(bf16[64,1024]{1,0:T(8,128)(2,1)S(1)} %constant_dynamic-update-slice_fusion.refs_0_), channel_id=1, source_target_pairs={{0,2},{1,3},{2,0},{3,1},{4,6},{5,7},{6,4},{7,5},{8,10},{9,11},{10,... | collective-permute-start | bytes 393224 | tf_op jit(solution)/shard_map/ppermute | solution.py:20
  43.6 4.6 %collective-permute-done.4.refs_1_ = bf16[32,10240]{1,0:T(8,128)(2,1)S(1)} collective-permute-done((bf16[32,10240]{1,0:T(8,128)(2,1)S(1)}, bf16[32,10240]{1,0:T(8,128)(2,1)S(1)}, u32[]{:S(2)}, u32[]{:S(2)}) %collective-permute-start.4) | collective-permute-done | bytes 655392 | tf_op jit(solution)/shard_map/ppermute | solution.py:20
  48.2 3.1 %collective-permute-start.14 = (f32[1,64,64]{2,1,0:T(8,128)S(1)}, f32[1,64,64]{2,1,0:T(8,128)S(1)}, u32[]{:S(2)}, u32[]{:S(2)}) collective-permute-start(f32[1,64,64]{2,1,0:T(8,128)S(1)} %slice.61), channel_id=1, source_target_pairs={{0,16},{4,20},{8,24},{12,28},{16,0},{20,4},{24,8},{28,12},{32,48},... | collective-permute-start | bytes 49160 | tf_op jit(solution)/shard_map/ppermute | solution.py:228
  51.2 0.0 collective-permute-done.5.refs_3_
  51.2 0.0 copy-done.5
  51.2 0.0 copy-start.1
  51.2 3.4 %copy-done.1 = bf16[32,8,64,256]{3,2,1,0:T(8,128)(2,1)S(1)} copy-done((bf16[32,8,64,256]{3,2,1,0:T(8,128)(2,1)S(1)}, bf16[32,8,64,256]{3,2,1,0:T(8,128)(2,1)}, u32[]{:S(2)}) %copy-start.1) | copy-done | bytes 8388632
  54.6 7.0 %near_sides.1 = (bf16[64,2048]{1,0:T(8,128)(2,1)}, bf16[64,2048]{1,0:T(8,128)(2,1)}) custom-call(s32[8,32]{1,0:T(8,128)S(1)} %bitcast.30, bf16[32,8,64,256]{3,2,1,0:T(8,128)(2,1)S(1)} %copy-done.1, bf16[32,8192]{1,0:T(8,128)(2,1)S(1)} %collective-permute-done.2.refs_2_.refs_0_, bf16[32,10240]{1,0:T(8,128)(2,1)S(1)} %collective-permute-done.4.refs_1_, ...), custom_call_target="tpu_custom_call" | custom-call | flops 1073741824 | bytes 8388608 | tf_op jit(solution)/shard_map/near_sides/pallas_call | solution.py:72
  61.7 0.0 copy-done.6
  61.7 0.1 collective-permute-start.6
  61.8 0.1 collective-permute-done.8.refs_0_
  61.9 0.0 slice-start
  61.9 1.4 %collective-permute-start.7 = (bf16[64,2048]{1,0:T(8,128)(2,1)}, bf16[64,2048]{1,0:T(8,128)(2,1)}, u32[]{:S(2)}, u32[]{:S(2)}) collective-permute-start(bf16[64,2048]{1,0:T(8,128)(2,1)} %get-tuple-element.6), channel_id=1, source_target_pairs={{0,1},{1,2},{2,3},{3,0},{4,5},{5,6},{6,7},{7,4},{8,9},{9,10},{10,1... | collective-permute-start | bytes 786440 | tf_op jit(solution)/shard_map/ppermute | solution.py:20
  63.2 0.0 collective-permute-done.10.refs_2_
  63.2 0.0 collective-permute-done.9.refs_1_
  63.2 4.6 %near_far.1 = bf16[64,2048]{1,0:T(8,128)(2,1)} custom-call(s32[8,32]{1,0:T(8,128)S(1)} %bitcast.31, bf16[32,8,64,256]{3,2,1,0:T(8,128)(2,1)S(1)} %copy-done.1, bf16[64,1024]{1,0:T(8,128)(2,1)S(1)} %collective-permute-done.8.refs_0_, bf16[32,8192]{1,0:T(8,128)(2,1)S(1)} %collective-permute-done.9.refs_1_, bf16[32,8192]{1,0:T(8,128)(2,1)S(1)} %collective-permute-done.10.refs_2_), custom_call_target="tpu_custom_call" | custom-call | flops 536870912 | bytes 8388608 | tf_op jit(solution)/shard_map/near_far/pallas_call | solution.py:72
  67.9 1.2 %collective-permute-start.11 = (bf16[64,2048]{1,0:T(8,128)(2,1)}, bf16[64,2048]{1,0:T(8,128)(2,1)}, u32[]{:S(2)}, u32[]{:S(2)}) collective-permute-start(bf16[64,2048]{1,0:T(8,128)(2,1)} %near_far.1), channel_id=1, source_target_pairs={{0,2},{1,3},{2,0},{3,1},{4,6},{5,7},{6,4},{7,5},{8,10},{9,11},{10,... | collective-permute-start | bytes 786440 | tf_op jit(solution)/shard_map/ppermute | solution.py:20
  69.1 0.0 collective-permute-done.14
  69.1 0.0 slice-done
  69.1 0.0 copy-start.3
  69.1 3.9 %near_own.1.refs_0_ = bf16[64,2048]{1,0:T(8,128)(2,1)S(1)} custom-call(s32[8,32]{1,0:T(8,128)S(1)} %bitcast.32, bf16[32,8,64,256]{3,2,1,0:T(8,128)(2,1)S(1)} %copy-done.1, bf16[64,1024]{1,0:T(8,128)(2,1)S(1)} %constant_dynamic-update-slice_fusion.refs_0_, bf16[64,8192]{1,0:T(8,128)(2,1)S(1)} %bitcast.28, ...), custom_call_target="tpu_custom_call" | custom-call | flops 536870912 | bytes 8388608 | tf_op jit(solution)/shard_map/near_own/pallas_call | solution.py:72
  73.1 0.0 all-to-all-done.everyone
  73.1 2.9 %coupled.1.refs_4_ = f32[64,64]{1,0:T(8,128)} custom-call(s32[1,8]{1,0:T(1,128)} %list_ref.1, bf16[8,64,64]{2,1,0:T(8,128)(2,1)} %bitcast.34, f32[64,32,128]{2,1,0:T(8,128)} %all-to-all-done.everyone), custom_call_target="tpu_custom_call" | custom-call | tf_op jit(solution)/shard_map/coupled/pallas_call | solution.py:164
  76.0 0.0 collective-permute-done.6.refs_1_
  76.0 0.0 collective-permute-done.7.refs_2_
  76.0 0.0 collective-permute-done.11.refs_3_
  76.0 0.0 copy-done.3
  76.0 0.0 copy-start.4
  76.0 0.7 copy-done.4
  76.8 3.0 %assemble.1 = bf16[64,8192]{1,0:T(8,128)(2,1)} custom-call(bf16[64,2048]{1,0:T(8,128)(2,1)S(1)} %near_own.1.refs_0_, bf16[64,2048]{1,0:T(8,128)(2,1)} %collective-permute-done.6.refs_1_, bf16[64,2048]{1,0:T(8,128)(2,1)} %collective-permute-done.7.refs_2_, bf16[64,2048]{1,0:T(8,128)(2,1)} %collective-permute-done.11.refs_3_, f32[64,64]{1,0:T(8,128)S(1)} %copy-done.4, ...), custom_call_target="tpu_custom_call" | custom-call | tf_op jit(solution)/shard_map/assemble/pallas_call | solution.py:128
  (10 shorter events, 0.1 us)
Async XLA Ops:
  0.6 12.5 %copy-start = (bf16[32,256,64]{1,2,0:T(8,128)(2,1)S(1)}, bf16[32,256,64]{1,2,0:T(8,128)(2,1)}, u32[]{:S(2)}) copy-start(bf16[32,256,64]{1,2,0:T(8,128)(2,1)} %param.11) | copy-start | bytes 3145732
  0.6 12.5 %copy-start.2 = (bf16[8192,64]{0,1:T(8,128)(2,1)S(1)}, bf16[8192,64]{0,1:T(8,128)(2,1)}, u32[]{:S(2)}) copy-start(bf16[8192,64]{0,1:T(8,128)(2,1)} %param.8) | copy-start | bytes 3145732
  1.7 27.9 %collective-permute-start = (bf16[64,512]{1,0:T(8,128)(2,1)S(1)}, bf16[64,512]{1,0:T(8,128)(2,1)S(1)}, u32[]{:S(2)}, u32[]{:S(2)}) collective-permute-start(bf16[64,512]{1,0:T(8,128)(2,1)S(1)} %get-tuple-element.10), channel_id=1, source_target_pairs={{0,4},{4,8},{8,12},{12,16},{16,20},{20,24},{24,28},{28,32},{32,36}... | collective-permute-start | bytes 196616 | tf_op jit(solution)/shard_map/ppermute | solution.py:26
  6.3 23.3 %collective-permute-start.1 = (bf16[64,512]{1,0:T(8,128)(2,1)S(1)}, bf16[64,512]{1,0:T(8,128)(2,1)S(1)}, u32[]{:S(2)}, u32[]{:S(2)}) collective-permute-start(bf16[64,512]{1,0:T(8,128)(2,1)S(1)} %get-tuple-element.9), channel_id=1, source_target_pairs={{4,0},{8,4},{12,8},{16,12},{20,16},{24,20},{28,24},{32,28},{36,32}... | collective-permute-start | bytes 196616 | tf_op jit(solution)/shard_map/ppermute | solution.py:26
  10.5 23.4 %collective-permute-start.2 = (bf16[32,8192]{1,0:T(8,128)(2,1)}, bf16[32,8192]{1,0:T(8,128)(2,1)S(1)}, u32[]{:S(2)}, u32[]{:S(2)}) collective-permute-start(bf16[32,8192]{1,0:T(8,128)(2,1)} %get-tuple-element.8), channel_id=1, source_target_pairs={{0,1},{1,2},{2,3},{3,0},{4,5},{5,6},{6,7},{7,4},{8,9},{9,10},{10,1... | collective-permute-start | bytes 1572872 | tf_op jit(solution)/shard_map/ppermute | solution.py:20
  11.7 22.1 %collective-permute-start.3 = (bf16[32,8192]{1,0:T(8,128)(2,1)}, bf16[32,8192]{1,0:T(8,128)(2,1)S(1)}, u32[]{:S(2)}, u32[]{:S(2)}) collective-permute-start(bf16[32,8192]{1,0:T(8,128)(2,1)} %get-tuple-element.7), channel_id=1, source_target_pairs={{0,3},{1,0},{2,1},{3,2},{4,7},{5,4},{6,5},{7,6},{8,11},{9,8},{10,9... | collective-permute-start | bytes 1572872 | tf_op jit(solution)/shard_map/ppermute | solution.py:20
  15.9 57.1 %all-to-all-start = ((f32[64,32,128]{2,1,0:T(8,128)}), f32[64,32,128]{2,1,0:T(8,128)}, u32[]{:S(2)}, u32[]{:S(2)}) async-start(f32[64,32,128]{2,1,0:T(8,128)} %broadcast_in_dim.12), calls=%async_computation | async-start | bytes 2097152 | tf_op jit(solution)/shard_map/all_to_all | solution.py:217
  29.7 5.6 %copy-start.7 = (bf16[3,1,64,64]{3,2,1,0:T(8,128)(2,1)S(1)}, bf16[3,1,64,64]{3,2,1,0:T(8,128)(2,1)}, u32[]{:S(2)}) copy-start(bf16[3,1,64,64]{3,2,1,0:T(8,128)(2,1)} %param.13) | copy-start | bytes 73732
  29.7 21.6 %copy-start.5 = (s32[32,8]{0,1:T(8,128)S(1)}, s32[32,8]{0,1:T(8,128)}, u32[]{:S(2)}) copy-start(s32[32,8]{0,1:T(8,128)} %param.10) | copy-start | bytes 3076
  31.0 17.2 %collective-permute-start.4 = (bf16[32,10240]{1,0:T(8,128)(2,1)S(1)}, bf16[32,10240]{1,0:T(8,128)(2,1)S(1)}, u32[]{:S(2)}, u32[]{:S(2)}) collective-permute-start(bf16[32,10240]{1,0:T(8,128)(2,1)S(1)} %get-tuple-element.12), channel_id=1, source_target_pairs={{0,1},{1,2},{2,3},{3,0},{4,5},{5,6},{6,7},{7,4},{8,9},{9,10},{10,1... | collective-permute-start | bytes 1966088 | tf_op jit(solution)/shard_map/ppermute | solution.py:20
  31.1 20.2 %collective-permute-start.5 = (bf16[32,10240]{1,0:T(8,128)(2,1)S(1)}, bf16[32,10240]{1,0:T(8,128)(2,1)S(1)}, u32[]{:S(2)}, u32[]{:S(2)}) collective-permute-start(bf16[32,10240]{1,0:T(8,128)(2,1)S(1)} %get-tuple-element.11), channel_id=1, source_target_pairs={{0,3},{1,0},{2,1},{3,2},{4,7},{5,4},{6,5},{7,6},{8,11},{9,8},{10,9... | collective-permute-start | bytes 1966088 | tf_op jit(solution)/shard_map/ppermute | solution.py:20
  33.8 29.5 %collective-permute-start.10 = (bf16[32,8192]{1,0:T(8,128)(2,1)S(1)}, bf16[32,8192]{1,0:T(8,128)(2,1)S(1)}, u32[]{:S(2)}, u32[]{:S(2)}) collective-permute-start(bf16[32,8192]{1,0:T(8,128)(2,1)S(1)} %collective-permute-done.3.refs_3_.refs_2_), channel_id=1, source_target_pairs={{0,3},{1,0},{2,1},{3,2},{4,7},{5,4},{6,5},{7,6},{8,11},{9,8},{10,9... | collective-permute-start | bytes 1572872 | tf_op jit(solution)/shard_map/ppermute | solution.py:20
  33.8 29.4 %collective-permute-start.9 = (bf16[32,8192]{1,0:T(8,128)(2,1)S(1)}, bf16[32,8192]{1,0:T(8,128)(2,1)S(1)}, u32[]{:S(2)}, u32[]{:S(2)}) collective-permute-start(bf16[32,8192]{1,0:T(8,128)(2,1)S(1)} %collective-permute-done.2.refs_2_.refs_0_), channel_id=1, source_target_pairs={{0,1},{1,2},{2,3},{3,0},{4,5},{5,6},{6,7},{7,4},{8,9},{9,10},{10,1... | collective-permute-start | bytes 1572872 | tf_op jit(solution)/shard_map/ppermute | solution.py:20
  35.5 2.7 %collective-permute-start.12 = (f32[3,64,64]{2,1,0:T(8,128)S(1)}, f32[3,64,64]{2,1,0:T(8,128)S(1)}, u32[]{:S(2)}, u32[]{:S(2)}) collective-permute-start(f32[3,64,64]{2,1,0:T(8,128)S(1)} %convolution_bitcast_fusion), channel_id=1, source_target_pairs={{0,4},{4,0},{8,12},{12,8},{16,20},{20,16},{24,28},{28,24},{32,36},... | collective-permute-start | bytes 147464 | tf_op jit(solution)/shard_map/ppermute | solution.py:228
  38.2 23.5 %copy-start.6 = (f32[3,64,64]{2,1,0:T(8,128)}, f32[3,64,64]{2,1,0:T(8,128)S(1)}, u32[]{:S(2)}) copy-start(f32[3,64,64]{2,1,0:T(8,128)S(1)} %add.9) | copy-start | bytes 147460
  38.2 4.6 %collective-permute-start.13 = (f32[2,64,64]{2,1,0:T(8,128)S(1)}, f32[2,64,64]{2,1,0:T(8,128)S(1)}, u32[]{:S(2)}, u32[]{:S(2)}) collective-permute-start(f32[2,64,64]{2,1,0:T(8,128)S(1)} %slice.59), channel_id=1, source_target_pairs={{0,8},{4,12},{8,0},{12,4},{16,24},{20,28},{24,16},{28,20},{32,40},... | collective-permute-start | bytes 98312 | tf_op jit(solution)/shard_map/ppermute | solution.py:228
  42.8 19.1 %collective-permute-start.8 = (bf16[64,1024]{1,0:T(8,128)(2,1)S(1)}, bf16[64,1024]{1,0:T(8,128)(2,1)S(1)}, u32[]{:S(2)}, u32[]{:S(2)}) collective-permute-start(bf16[64,1024]{1,0:T(8,128)(2,1)S(1)} %constant_dynamic-update-slice_fusion.refs_0_), channel_id=1, source_target_pairs={{0,2},{1,3},{2,0},{3,1},{4,6},{5,7},{6,4},{7,5},{8,10},{9,11},{10,... | collective-permute-start | bytes 393224 | tf_op jit(solution)/shard_map/ppermute | solution.py:20
  48.2 20.9 %collective-permute-start.14 = (f32[1,64,64]{2,1,0:T(8,128)S(1)}, f32[1,64,64]{2,1,0:T(8,128)S(1)}, u32[]{:S(2)}, u32[]{:S(2)}) collective-permute-start(f32[1,64,64]{2,1,0:T(8,128)S(1)} %slice.61), channel_id=1, source_target_pairs={{0,16},{4,20},{8,24},{12,28},{16,0},{20,4},{24,8},{28,12},{32,48},... | collective-permute-start | bytes 49160 | tf_op jit(solution)/shard_map/ppermute | solution.py:228
  51.2 3.4 %copy-start.1 = (bf16[32,8,64,256]{3,2,1,0:T(8,128)(2,1)S(1)}, bf16[32,8,64,256]{3,2,1,0:T(8,128)(2,1)}, u32[]{:S(2)}) copy-start(bf16[32,8,64,256]{3,2,1,0:T(8,128)(2,1)} %blocks_ref.5) | copy-start | bytes 25165828
  61.7 14.3 %collective-permute-start.6 = (bf16[64,2048]{1,0:T(8,128)(2,1)}, bf16[64,2048]{1,0:T(8,128)(2,1)}, u32[]{:S(2)}, u32[]{:S(2)}) collective-permute-start(bf16[64,2048]{1,0:T(8,128)(2,1)} %get-tuple-element.5), channel_id=1, source_target_pairs={{0,3},{1,0},{2,1},{3,2},{4,7},{5,4},{6,5},{7,6},{8,11},{9,8},{10,9... | collective-permute-start | bytes 786440 | tf_op jit(solution)/shard_map/ppermute | solution.py:20
  61.9 7.2 %slice-start = ((f32[3,64,64]{2,1,0:T(8,128)}), f32[1,64,64]{2,1,0:T(8,128)S(1)}, s32[]{:S(2)}) async-start(f32[3,64,64]{2,1,0:T(8,128)} %copy-done.6), calls=%async_computation.1 | async-start | bytes 65536 | tf_op jit(solution)/shard_map/slice | solution.py:229
  61.9 14.1 %collective-permute-start.7 = (bf16[64,2048]{1,0:T(8,128)(2,1)}, bf16[64,2048]{1,0:T(8,128)(2,1)}, u32[]{:S(2)}, u32[]{:S(2)}) collective-permute-start(bf16[64,2048]{1,0:T(8,128)(2,1)} %get-tuple-element.6), channel_id=1, source_target_pairs={{0,1},{1,2},{2,3},{3,0},{4,5},{5,6},{6,7},{7,4},{8,9},{9,10},{10,1... | collective-permute-start | bytes 786440 | tf_op jit(solution)/shard_map/ppermute | solution.py:20
  67.9 8.1 %collective-permute-start.11 = (bf16[64,2048]{1,0:T(8,128)(2,1)}, bf16[64,2048]{1,0:T(8,128)(2,1)}, u32[]{:S(2)}, u32[]{:S(2)}) collective-permute-start(bf16[64,2048]{1,0:T(8,128)(2,1)} %near_far.1), channel_id=1, source_target_pairs={{0,2},{1,3},{2,0},{3,1},{4,6},{5,7},{6,4},{7,5},{8,10},{9,11},{10,... | collective-permute-start | bytes 786440 | tf_op jit(solution)/shard_map/ppermute | solution.py:20
  69.1 6.9 %copy-start.3 = (f32[3,1,64,64]{3,2,1,0:T(8,128)}, f32[3,1,64,64]{3,2,1,0:T(8,128)S(1)}, u32[]{:S(2)}) copy-start(f32[3,1,64,64]{3,2,1,0:T(8,128)S(1)} %maximum_bitcast_fusion.refs_5_) | copy-start | bytes 147460
  76.0 0.8 copy-start.4
